TPU v7x, 32 devices: a whole 2x2x4 slice. The times are simulated.
32 devices in a mesh: blk: 32 (over z, y, x, core), seq: 1, mp: 1.
Axes of the slice: x: 2, y: 2, z: 4, core: 2. Of those that a mesh axis runs over, the one named last changes fastest.
Arguments:
- hidden: bfloat16 [1, 512, 1536], P(('mp', 'seq'), 'blk'), may hold values from -6 to 6
- labels: int32 [1, 512], P('seq'), may hold values from 0 to 25151
- lengths: int32 [1, 8], P('seq'), may hold values from 1 to 256, 512 in all within a row
- owners: int32 [8], replicated, may hold values from 0 to 7, each once
- w_inner: bfloat16 [1536, 2, 1536], P('mp', None, 'blk'), may hold values from -0.15625 to 0.15625
- w_bcdt: bfloat16 [1536, 280], P('mp'), may hold values from -0.15625 to 0.15625
- conv_inner: float32 [4, 1536], P('mp', 'blk'), may hold values from -3 to 3
- conv_bc: float32 [4, 256], P('mp'), may hold values from -3 to 3
- dt_bias: float32 [24], P('mp'), may hold values from -3 to 0.5
- decay_rate: float32 [24], P('mp'), may hold values from 0.01 to 1
- d_skip: float32 [24], P('mp'), may hold values from 0.5 to 2
- norm_gain: float32 [1536], P(('mp', 'blk')), may hold values from 0.5 to 1.5
- w_out: bfloat16 [1536, 1536], P(('mp', 'blk')), may hold values from -0.15625 to 0.15625
- final_gain: float32 [1536], P('mp'), may hold values from 0.5 to 1.5
- w_head: bfloat16 [1536, 25152], P('mp', 'blk'), may hold values from -0.33170174 to 0.33170174
Outputs:
- layer_out: bfloat16 [1, 512, 1536], P(('mp', 'seq'), 'blk')
- token_logprob: float32 [1, 512], P(('mp', 'seq'), 'blk')
- seq_logprob: float32 [8], P(('mp', 'seq'))
Inputs may be any that keep to these rules, and one draw needn't show every extreme that they name: The 8 lengths of a group sum to 512 and the longest is exactly 256. `owners`: every output slot is named once.
All inputs are finite; a program needn't handle non-finite values.
Results may differ from a plain program's by a relative error of at most 0.0055.
Values may be sent and summed in bfloat16 or wider, within the bound.
A program may use at most 64 MiB of HBM per device.

v0:
```python
import jax
import jax.numpy as jnp
from jax import lax
from jax.sharding import PartitionSpec as P

D = 1536
HEADDIM = 64
NSTATE = 128
SCAN_BLOCK = 256
CONV = 4


EPSILON = 1e-05
HIGH = lax.Precision.HIGHEST


def segments_of(lengths, count):
    starts = jnp.cumsum(lengths, axis=-1) - lengths
    places = jnp.arange(count, dtype=jnp.int32)
    segment = jnp.sum((places[:, None] >= starts[None, :]).astype(jnp.int32), axis=-1) - 1
    first = jnp.take(starts, segment)
    return (segment, places - first)


def causal_conv(values, weights, position):
    total = values * weights[0]
    for shift_by in range(1, CONV):
        moved = jnp.concatenate(
            [jnp.zeros_like(values[:shift_by, :]), values[:-shift_by, :]], axis=0
        )
        total = (
            total + moved * weights[shift_by] * (position >= shift_by).astype(jnp.float32)[:, None]
        )
    return total


def final_norm(values, gain):
    widened = values.astype(jnp.float32)
    scale = lax.rsqrt(jnp.mean(widened * widened, axis=-1, keepdims=True) + EPSILON)
    return (widened * scale * gain).astype(jnp.bfloat16)


def shards(
    hidden,
    labels,
    lengths,
    owners,
    w_inner,
    w_bcdt,
    conv_inner,
    conv_bc,
    dt_bias,
    decay_rate,
    d_skip,
    norm_gain,
    w_out,
    final_gain,
    w_head,
):
    rows_own = hidden[0]
    rows_count = rows_own.shape[0]
    blk_count = lax.axis_size("blk")
    blk_index = lax.axis_index("blk")
    gathered = lax.all_gather(rows_own, "blk", axis=0, tiled=True)
    tokens_all = gathered.shape[0]
    channels = w_inner.shape[2]
    inner_total = channels * blk_count
    inner_proj = jnp.dot(
        gathered, w_inner.reshape(D, 2 * channels), preferred_element_type=jnp.float32
    ).astype(jnp.bfloat16)
    state_proj = jnp.dot(gathered, w_bcdt, preferred_element_type=jnp.float32).astype(jnp.bfloat16)
    gate_half = inner_proj[:, :channels].astype(jnp.float32)
    segment, position = segments_of(lengths[0], tokens_all)
    conv_value = jax.nn.silu(
        causal_conv(inner_proj[:, channels:].astype(jnp.float32), conv_inner, position)
    )
    conv_state = jax.nn.silu(
        causal_conv(state_proj[:, : 2 * NSTATE].astype(jnp.float32), conv_bc, position)
    )
    input_map = conv_state[:, :NSTATE]
    output_map = conv_state[:, NSTATE:]
    step_size = jax.nn.softplus(state_proj[:, 2 * NSTATE :].astype(jnp.float32) + dt_bias)
    log_heads = -(step_size * decay_rate)
    first_channel = blk_index * channels
    channel_head = (first_channel + jnp.arange(channels, dtype=jnp.int32)) // HEADDIM
    head_low = first_channel // HEADDIM
    head_high = (first_channel + channels - 1) // HEADDIM
    mask_high = (channel_head == head_high).astype(jnp.float32)
    mask_low = 1.0 - mask_high
    step_pair = jnp.concatenate(
        [
            lax.dynamic_slice_in_dim(step_size, head_low, 1, 1),
            lax.dynamic_slice_in_dim(step_size, head_high, 1, 1),
        ],
        axis=1,
    )
    log_pair = jnp.concatenate(
        [
            lax.dynamic_slice_in_dim(log_heads, head_low, 1, 1),
            lax.dynamic_slice_in_dim(log_heads, head_high, 1, 1),
        ],
        axis=1,
    )
    step_channel = step_pair[:, 0:1] * mask_low + step_pair[:, 1:2] * mask_high
    driven = conv_value * step_channel
    slot_masks = (mask_low, mask_high)
    blocks = tokens_all // SCAN_BLOCK
    order = jnp.arange(SCAN_BLOCK, dtype=jnp.int32)
    causal = order[:, None] >= order[None, :]

    def block_step(carry, inputs):
        carried, previous = carry
        drive_block, in_block, out_block, log_block, seg_block = inputs
        cumulative = jnp.cumsum(log_block, axis=0)
        gram = jnp.dot(out_block, in_block.T, precision=HIGH)
        same = (seg_block[:, None] == seg_block[None, :]) & causal
        result = jnp.zeros((SCAN_BLOCK, channels), jnp.float32)
        for slot_index in range(2):
            column = cumulative[:, slot_index]
            spread = jnp.minimum(column[:, None] - column[None, :], 0.0)
            weights = jnp.where(same, jnp.exp(spread), 0.0)
            result = result + jnp.dot(
                gram * weights, drive_block * slot_masks[slot_index], precision=HIGH
            )
        carried_in = carried * (seg_block[0] == previous).astype(jnp.float32)
        rising = jnp.exp(cumulative[:, 0:1]) * mask_low + jnp.exp(cumulative[:, 1:2]) * mask_high
        leading = (seg_block == seg_block[0]).astype(jnp.float32)[:, None]
        result = result + leading * rising * jnp.dot(out_block, carried_in.T, precision=HIGH)
        trailing = (seg_block == seg_block[-1]).astype(jnp.float32)[:, None]
        tail_low = jnp.exp(cumulative[-1:, 0:1] - cumulative[:, 0:1])
        tail_high = jnp.exp(cumulative[-1:, 1:2] - cumulative[:, 1:2])
        tail = tail_low * mask_low + tail_high * mask_high
        whole_block = (seg_block[-1] == seg_block[0]).astype(jnp.float32)
        carried_new = whole_block * rising[-1][:, None] * carried_in + jnp.dot(
            (drive_block * tail * trailing).T, in_block, precision=HIGH
        )
        return ((carried_new, seg_block[-1]), result)

    initial = (jnp.zeros((channels, NSTATE), jnp.float32), jnp.int32(-1))
    scan_inputs = (
        driven.reshape(blocks, SCAN_BLOCK, channels),
        input_map.reshape(blocks, SCAN_BLOCK, NSTATE),
        output_map.reshape(blocks, SCAN_BLOCK, NSTATE),
        log_pair.reshape(blocks, SCAN_BLOCK, 2),
        segment.reshape(blocks, SCAN_BLOCK),
    )
    final_carry, scanned = lax.scan(block_step, initial, scan_inputs)
    mixed = scanned.reshape(tokens_all, channels) + jnp.take(d_skip, channel_head) * conv_value
    gated = mixed * jax.nn.silu(gate_half)
    squares = lax.psum(jnp.sum(gated * gated, axis=1), "blk")
    inverse = lax.rsqrt(squares / inner_total + EPSILON)
    gated_norm = (gated * inverse[:, None] * norm_gain).astype(jnp.bfloat16)
    delta_own = lax.psum_scatter(
        jnp.dot(gated_norm, w_out, preferred_element_type=jnp.float32),
        "blk",
        scatter_dimension=0,
        tiled=True,
    )
    layer_own = (rows_own.astype(jnp.float32) + delta_own).astype(jnp.bfloat16)
    logits = jnp.dot(
        lax.all_gather(final_norm(layer_own, final_gain), "blk", axis=0, tiled=True),
        w_head,
        preferred_element_type=jnp.float32,
    )
    vocab_local = w_head.shape[1]
    local_label = labels[0] - blk_index * vocab_local
    hit = jnp.arange(vocab_local, dtype=jnp.int32)[None, :] == local_label[:, None]
    target_local = jnp.sum(jnp.where(hit, logits, 0.0), axis=1)
    top_local = jnp.max(logits, axis=1)
    top_all = lax.pmax(top_local, "blk")
    expsum_local = jnp.sum(jnp.exp(logits - top_all[:, None]), axis=1)
    expsum_all, target_all = lax.psum((expsum_local, target_local), "blk")
    logprob = target_all - (top_all + jnp.log(expsum_all))
    token_own = lax.dynamic_slice_in_dim(logprob, blk_index * rows_count, rows_count, 0)
    seqs_count = lengths.shape[1]
    onehot = (segment[:, None] == jnp.arange(seqs_count, dtype=jnp.int32)[None, :]).astype(
        jnp.float32
    )
    sums = jnp.dot(logprob, onehot, precision=HIGH)
    seq_index = lax.axis_index("seq")
    mine = lax.dynamic_slice_in_dim(owners, seq_index * seqs_count, seqs_count, 0)
    placement = (mine[:, None] == jnp.arange(owners.shape[0], dtype=jnp.int32)[None, :]).astype(
        jnp.float32
    )
    spread_sums = jnp.dot(sums, placement, precision=HIGH)
    seq_own = lax.psum_scatter(spread_sums, "seq", scatter_dimension=0, tiled=True)
    return (layer_own[None], token_own[None], seq_own)


def solution(mesh):
    in_specs = (
        P(("mp", "seq"), "blk", None),
        P("seq", None),
        P("seq", None),
        P(),
        P("mp", None, "blk"),
        P("mp", None),
        P("mp", "blk"),
        P("mp", None),
        P("mp"),
        P("mp"),
        P("mp"),
        P(("mp", "blk")),
        P(("mp", "blk"), None),
        P("mp"),
        P("mp", "blk"),
    )
    out_specs = (P(("mp", "seq"), "blk", None), P(("mp", "seq"), "blk"), P(("mp", "seq")))
    return jax.shard_map(shards, mesh=mesh, in_specs=in_specs, out_specs=out_specs, check_vma=False)
```

profile of v0, /device:TPU:0, one launch (start us, length us, event | category | flops | bytes accessed | tf_op | source)
XLA Modules:
  0.0 395.0 jit_solution(14176987990005490306)
XLA Ops:
  7.2 0.7 all-gather.6.cloned.1.call-update
  8.0 0.8 reduce-window.10
  8.8 0.7 fusion.92
  9.6 1.4 gather_fusion
  11.1 0.7 bitcast_subtract_fusion
  11.7 0.7 fusion.100
  12.4 0.6 broadcast_subtract_fusion.2
  13.0 1.4 slice_bitcast_fusion.3
  14.4 4.5 %compare_select_fusion.5 = s32[512,1]{0,1:T(1,128)S(1)} fusion(s32[]{:T(128)} %bitcast.14, s32[]{:T(128)} %bitcast.15, s32[]{:T(128)} %bitcast.16, s32[]{:T(128)} %bitcast.17, s32[]{:T(128)} %bitcast.18, s32[]{:T(128)} %bitcast.20, s32[]{:T(128)} %bitcast.19, s32[512,1]{0,1:T(1,128)S(1)} %bitcast.206, s32[512,1]{0,1:T(1,128)S(1)} %bitcast.202), kind=kLoop, calls=%fused_computation.133 | loop fusion | flops 7168 | bytes 6172 | tf_op jit(solution)/shard_map/jit(_take)/gather | solution.py:21
  19.0 0.6 compare_convert_fusion.5
  19.6 0.8 fusion.99
  20.4 48.1 %all-gather.6.cloned.1.call-done = bf16[1,512,1536]{2,1,0:T(8,128)(2,1)} async-done(((bf16[1,16,1536]{2,1,0:T(8,128)(2,1)}), bf16[1,512,1536]{2,1,0:T(8,128)(2,1)}) %all-gather.6.cloned.1.call-update) | async-done | bytes 1572880 | tf_op jit(solution)/shard_map/all_gather | solution.py:64
  68.6 2.3 fusion.71
  70.9 0.7 divide_multiply_fusion
  71.9 2.0 fusion.74
  74.0 0.8 compare_select_fusion.3
  74.8 0.9 add_multiply_fusion
  75.8 24.4 %while.17 = (s32[]{:T(128)}, f32[48,128]{1,0:T(8,128)S(1)}, s32[]{:T(128)}, f32[2,256,48]{1,0,2:T(2,128)}, s32[2,256]{1,0:T(2,128)S(1)}, /*index=5*/f32[2,256,2]...) while((s32[]{:T(128)}, f32[48,128]{1,0:T(8,128)S(1)}, ...), condition=%wide.region_5.6_spmd.clone.clone.clone, body=%wide.region_2.5_spmd.clone.clone.clone.sunk | while | flops 215140816 | bytes 2173324 | solution.py:147
  75.8 0.6 reduce-window.24
  76.8 0.7 fusion.129
  77.5 1.3 fusion.130
  78.8 0.4 fusion.132
  79.3 0.5 fusion.133
  79.7 0.5 convolution_add_fusion.5
  80.2 0.6 constant_dynamic-slice_fusion.12
  80.8 1.3 compare_convert_fusion.10
  83.2 2.2 dynamic_update_slice.8
  88.0 0.6 reduce-window.24
  89.0 0.7 fusion.129
  89.7 1.3 fusion.130
  91.4 0.5 fusion.133
  91.9 0.5 convolution_add_fusion.5
  92.4 0.6 constant_dynamic-slice_fusion.12
  93.0 1.3 compare_convert_fusion.10
  95.4 2.2 dynamic_update_slice.8
  100.1 0.9 copy.49
  101.1 38.9 %psum.21 = f32[512]{0:T(512)S(1)} all-reduce(f32[512]{0:T(512)S(1)} %get-tuple-element.240), channel_id=1, replica_groups=mesh['blk'=32,'seq'=1,'mp'=1] {'blk'}, use_global_device_ids=true, to_apply=%region_7.8 | all-reduce | flops 512 | bytes 4096 | tf_op jit(solution)/shard_map/psum | solution.py:150
  140.1 3.2 fusion.86
  143.4 101.6 %reduce-scatter.2.cloned.1.call-done = f32[16,1536]{1,0:T(8,128)} async-done(((f32[512,1536]{1,0:T(8,128)}), f32[16,1536]{1,0:T(8,128)}) %reduce-scatter.2.cloned.1.call-update) | async-done | bytes 98320 | tf_op jit(solution)/shard_map/reduce_scatter | solution.py:153
  245.0 1.0 fusion.82
  246.0 0.7 fusion.84
  246.8 55.0 %all-gather.4.cloned.1.call-done = bf16[512,1536]{1,0:T(8,128)(2,1)} async-done(((bf16[16,1536]{1,0:T(8,128)(2,1)}), bf16[512,1536]{1,0:T(8,128)(2,1)}) %all-gather.4.cloned.1.call-update) | async-done | bytes 1572880 | tf_op jit(solution)/shard_map/all_gather | solution.py:161
  301.8 4.1 %fusion.101 = (f32[512]{0:T(512)S(1)}, f32[512,786]{0,1:T(8,128)}) fusion(bf16[512,1536]{1,0:T(8,128)(2,1)} %all-gather.4.cloned.1.call-done, bf16[1536,786]{0,1:T(8,128)(2,1)S(1)} %copy-done), kind=kOutput, calls=%fused_computation.186 | convolution fusion | flops 1236673024 | bytes 5599232 | tf_op jit(solution)/shard_map/dot_general | solution.py:160
  305.9 38.8 %pmax.7 = f32[512]{0:T(512)S(1)} all-reduce(f32[512]{0:T(512)S(1)} %get-tuple-element.288), channel_id=1, replica_groups=mesh['blk'=32,'seq'=1,'mp'=1] {'blk'}, use_global_device_ids=true, to_apply=%region_13.14 | all-reduce | flops 512 | bytes 4096 | tf_op jit(solution)/shard_map/pmax | solution.py:170
  344.7 1.9 exponential_reduce_fusion
  346.6 40.3 %all-reduce.6 = (f32[512]{0:T(512)S(1)}, f32[512]{0:T(512)S(1)}) all-reduce(f32[512]{0:T(512)S(1)} %get-tuple-element.211, f32[512]{0:T(512)S(1)} %get-tuple-element.210), channel_id=1, replica_groups=mesh['blk'=32,'seq'=1,'mp'=1] {'blk'}, use_global_device_ids=true, to_apply=%region_11.12 | all-reduce | flops 1024 | bytes 8192 | tf_op jit(solution)/shard_map/psum | solution.py:172
  387.2 0.6 dynamic-slice_bitcast_fusion.1
  387.8 0.7 convolution_bitcast_fusion.1
  (71 shorter events, 4.3 us)
Async XLA Ops:
  7.2 294.7 %copy-start = (bf16[1536,786]{0,1:T(8,128)(2,1)S(1)}, bf16[1536,786]{0,1:T(8,128)(2,1)}, u32[]{:S(2)}) copy-start(bf16[1536,786]{0,1:T(8,128)(2,1)} %param.31) | copy-start | bytes 7243780
  7.2 61.4 %all-gather.6.cloned.1.call-start = ((), (), s32[]{:S(2)}) async-start(), calls=%async_computation.3 | async-start | bytes 1622016 | tf_op jit(solution)/shard_map/all_gather | solution.py:64
  7.9 237.1 %reduce-scatter.2.cloned.1.call-start = ((), (), s32[]{:S(2)}) async-start(), calls=%async_computation.1 | async-start | bytes 3244032 | tf_op jit(solution)/shard_map/reduce_scatter | solution.py:153
  75.7 64.3 %copy-start.5 = (f32[48]{0:T(128)S(1)}, f32[48]{0:T(128)}, u32[]{:S(2)}) copy-start(f32[48]{0:T(128)} %param.28) | copy-start | bytes 580
  143.3 101.7 %copy-start.1 = (bf16[1,16,1536]{2,1,0:T(8,128)(2,1)S(1)}, bf16[1,16,1536]{2,1,0:T(8,128)(2,1)}, u32[]{:S(2)}) copy-start(bf16[1,16,1536]{2,1,0:T(8,128)(2,1)} %param.17) | copy-start | bytes 147460
  143.3 102.7 %copy-start.3 = (f32[1536]{0:T(1024)S(1)}, f32[1536]{0:T(1024)}, u32[]{:S(2)}) copy-start(f32[1536]{0:T(1024)} %param.30) | copy-start | bytes 18436
  143.3 103.5 %copy-start.4 = (s32[1,512]{1,0:T(1,128)S(1)}, s32[1,512]{1,0:T(1,128)}, u32[]{:S(2)}) copy-start(s32[1,512]{1,0:T(1,128)} %param.18) | copy-start | bytes 6148
  143.3 158.5 %all-gather.4.cloned.1.call-start = ((), (), s32[]{:S(2)}) async-start(), calls=%async_computation.2 | async-start | bytes 1622016 | tf_op jit(solution)/shard_map/all_gather | solution.py:161
  246.0 59.9 %copy-start.2 = (bf16[16,1536]{1,0:T(8,128)(2,1)}, bf16[16,1536]{1,0:T(8,128)(2,1)S(1)}, u32[]{:S(2)}) copy-start(bf16[16,1536]{1,0:T(8,128)(2,1)S(1)} %get-tuple-element.239) | copy-start | bytes 147460
  305.9 81.9 %copy-start.6 = (s32[8]{0:T(128)S(1)}, s32[8]{0:T(128)}, u32[]{:S(2)}) copy-start(s32[8]{0:T(128)} %param.20) | copy-start | bytes 100
Sparse Core Ops, SparseCore 0:
  10.9 57.6 all-gather.5
  143.4 101.4 reduce-scatter.1
  247.9 53.9 all-gather.3
where the time goes:
time: 396 us; the launch traced here: 395 us
  waiting for transfers between devices  205 us (52%)
  blocking collectives  118 us (30%)
  other arithmetic  21.6 us (5%)
  matrix products  16.3 us (4%)
  between operations  14 us (4%)
  local copies, waits for them, and re-layouts  13.9 us (4%)
  loops' own time  5.61 us (1%)
    reduce_scatter x1, waiting for transfers between devices, shards(): lax.psum_scatter(jnp.dot(gated_norm, w_out, preferred_element_type=jnp.fl...  102 us
    all_gather x1, waiting for transfers between devices, shards(): lax.all_gather(final_norm(layer_own, final_gain), 'blk', axis=0, tiled=True)  55 us
    all_gather x1, waiting for transfers between devices, shards(): gathered = lax.all_gather(rows_own, 'blk', axis=0, tiled=True)  48.1 us
    psum x1, blocking collectives, shards(): expsum_all, target_all = lax.psum((expsum_local, target_local), 'blk')  40.3 us
    psum x1, blocking collectives, shards(): squares = lax.psum(jnp.sum(gated * gated, axis=1), 'blk')  38.9 us
    pmax x1, blocking collectives, shards(): top_all = lax.pmax(top_local, 'blk')  38.8 us
  transfers between devices with their start and end apart: 3, of which 3 were waited for; matrix products, arithmetic and copies ran while one was open for 3% of the time, Pallas kernels for 0%

commit v1 on v0

--- a/solution.py
+++ b/solution.py
@@ -1,6 +1,10 @@
+import functools
+
 import jax
 import jax.numpy as jnp
 from jax import lax
+from jax.experimental import pallas as pl
+from jax.experimental.pallas import tpu as pltpu
 from jax.sharding import PartitionSpec as P
 
 D = 1536
@@ -15,7 +19,9 @@
 
 
 def segments_of(lengths, count):
-    starts = jnp.cumsum(lengths, axis=-1) - lengths
+    order = jnp.arange(lengths.shape[0], dtype=jnp.int32)
+    earlier = order[None, :] < order[:, None]
+    starts = jnp.sum(jnp.where(earlier, lengths[None, :], 0), axis=-1)
     places = jnp.arange(count, dtype=jnp.int32)
     segment = jnp.sum((places[:, None] >= starts[None, :]).astype(jnp.int32), axis=-1) - 1
     first = jnp.take(starts, segment)
@@ -111,7 +117,7 @@
     def block_step(carry, inputs):
         carried, previous = carry
         drive_block, in_block, out_block, log_block, seg_block = inputs
-        cumulative = jnp.cumsum(log_block, axis=0)
+        cumulative = jnp.dot(causal.astype(jnp.float32), log_block, precision=HIGH)
         gram = jnp.dot(out_block, in_block.T, precision=HIGH)
         same = (seg_block[:, None] == seg_block[None, :]) & causal
         result = jnp.zeros((SCAN_BLOCK, channels), jnp.float32)
@@ -187,6 +193,482 @@
     return (layer_own[None], token_own[None], seq_own)
 
 
+LANES = 128
+PLANES = 4
+NT = (((1,), (1,)), ((), ()))
+F32 = jnp.float32
+BF16 = jnp.bfloat16
+
+
+def iota(shape, dim):
+    return lax.broadcasted_iota(jnp.int32, shape, dim)
+
+
+def remote(source, target, send_sem, recv_sem, device):
+    return pltpu.make_async_remote_copy(
+        src_ref=source,
+        dst_ref=target,
+        send_sem=send_sem,
+        recv_sem=recv_sem,
+        device_id={"blk": device},
+        device_id_type=pl.DeviceIdType.MESH,
+    )
+
+
+class Gather:
+    def __init__(self, buf, z_sem, p_sem, c_sem, recv_sem, count, me):
+        self.buf, self.z_sem, self.p_sem, self.c_sem, self.recv_sem = buf, z_sem, p_sem, c_sem, recv_sem
+        self.me, self.planes, self.width = me, PLANES, count // (2 * PLANES)
+        self.core = me % 2
+        self.spot = (me // 2) % self.width
+        self.plane = me // (2 * self.width)
+        self.sibling = me + 1 - 2 * self.core
+
+    def index(self, plane, spot, core):
+        return (plane * self.width + spot) * 2 + core
+
+    def copy(self, block, send_sem, device):
+        return remote(self.buf.at[block], self.buf.at[block], send_sem, self.recv_sem.at[block], device)
+
+    def plane_at(self, step):
+        return (self.plane + step) % self.planes
+
+    def spot_at(self, step):
+        return (self.spot + step) % self.width
+
+    def to_plane(self, block, step):
+        def one(d, carry):
+            device = self.index(self.plane, self.spot_at(d), self.core)
+            self.copy(block, self.p_sem.at[step * (self.width - 1) + d - 1], device).start()
+            return carry
+
+        lax.fori_loop(1, self.width, one, 0)
+
+    def to_core(self, block, slot):
+        self.copy(block, self.c_sem.at[slot], self.sibling).start()
+
+    def start(self):
+        def one(d, carry):
+            device = self.index(self.plane_at(d), self.spot, self.core)
+            self.copy(self.me, self.z_sem.at[d - 1], device).start()
+            return carry
+
+        lax.fori_loop(1, self.planes, one, 0)
+        self.to_plane(self.me, 0)
+        self.to_core(self.me, 0)
+
+    def arrived(self, block):
+        self.copy(block, self.c_sem.at[0], self.sibling).wait_recv()
+
+    def forward(self):
+        def along(d, carry):
+            block = self.index(self.plane_at(d), self.spot, self.core)
+            self.arrived(block)
+            self.to_plane(block, d)
+            self.to_core(block, d)
+            return carry
+
+        lax.fori_loop(1, self.planes, along, 0)
+
+        def within(i, carry):
+            step, d = i // (self.width - 1), i % (self.width - 1) + 1
+            block = self.index(self.plane_at(step), self.spot_at(d), self.core)
+            self.arrived(block)
+            self.to_core(block, self.planes + i)
+            return carry
+
+        lax.fori_loop(0, self.planes * (self.width - 1), within, 0)
+
+    def finish(self):
+        def last(i, carry):
+            block = self.index(i // self.width, i % self.width, 1 - self.core)
+            self.arrived(block)
+            return carry
+
+        lax.fori_loop(0, self.planes * self.width, last, 0)
+
+    def drain(self):
+        for sem, number in (
+            (self.z_sem, self.planes - 1),
+            (self.p_sem, self.planes * (self.width - 1)),
+            (self.c_sem, self.planes * self.width),
+        ):
+            def one(i, carry, sem=sem):
+                self.copy(self.me, sem.at[i], self.sibling).wait_send()
+                return carry
+
+            lax.fori_loop(0, number, one, 0)
+
+
+def silu(x):
+    return x * jax.nn.sigmoid(x)
+
+
+def rolled_conv(values, taps, position):
+    total = values * taps[0:1]
+    for shift_by in range(1, CONV):
+        moved = pltpu.roll(values, shift_by, 0)
+        total = total + jnp.where(position >= shift_by, moved * taps[shift_by : shift_by + 1], 0.0)
+    return total
+
+
+def pick(row, index):
+    lanes = iota(row.shape, 1)
+    return jnp.sum(jnp.where(lanes == index, row, 0.0), axis=1, keepdims=True)
+
+
+def column_of(row):
+    size = row.shape[1]
+    same = iota((size, size), 0) == iota((size, size), 1)
+    return jnp.sum(jnp.where(same, row, 0.0), axis=1, keepdims=True)
+
+
+def kernel(
+    count,
+    hidden,
+    labels,
+    lengths,
+    owners,
+    w_inner,
+    w_bcdt,
+    conv_inner,
+    conv_bc,
+    dt_bias,
+    decay_rate,
+    d_skip,
+    norm_gain,
+    w_out,
+    final_gain,
+    w_head,
+    layer_out,
+    token_out,
+    seq_out,
+    h_buf,
+    g_buf,
+    l_buf,
+    w_src,
+    w_dst,
+    f_buf,
+    wide,
+    heads,
+    tail,
+    heads_t,
+    scores,
+    h_z, h_p, h_c, h_r,
+    g_z, g_p, g_c, g_r,
+    l_z, l_p, l_c, l_r,
+    w_s, w_r,
+    f_s, f_r,
+    head_sem,
+):
+    me = lax.axis_index("blk")
+    rows = hidden.shape[0]
+    depth = hidden.shape[1]
+    tokens = rows * count
+    channels = w_inner.shape[1] // 2
+    columns = depth // count
+    vocab = w_head.shape[1]
+    padded = heads_t.shape[0]
+
+    fetch = pltpu.make_async_copy(w_head, heads, head_sem)
+    fetch.start()
+    h_buf[me] = hidden[...]
+
+    barrier = pltpu.get_barrier_semaphore()
+
+    def greet(d, carry):
+        pl.semaphore_signal(
+            barrier, inc=1, device_id={"blk": (me + d) % count}, device_id_type=pl.DeviceIdType.MESH
+        )
+        return carry
+
+    lax.fori_loop(1, count, greet, 0)
+    pl.semaphore_wait(barrier, count - 1)
+
+    h_all = Gather(h_buf, h_z, h_p, h_c, h_r, count, me)
+    h_all.start()
+
+    wide[...] = w_out[...].astype(F32) * column_of(norm_gain[...])
+    for e in range(count):
+        w_src[e, :, 0:columns] = wide[:, e * columns : (e + 1) * columns].astype(BF16)
+    h_all.forward()
+
+    def give(d, carry):
+        device = (me + d) % count
+        remote(w_src.at[device], w_dst.at[me], w_s.at[d], w_r.at[d], device).start()
+        return carry
+
+    lax.fori_loop(1, count, give, 0)
+    w_dst[me] = w_src[me]
+
+    places = lengths.shape[1]
+    length_row = lengths[...].astype(F32)
+    length_col = column_of(length_row)
+    later = iota((places, places), 0) < iota((places, places), 1)
+    starts_row = jnp.sum(jnp.where(later, length_col, 0.0), axis=0, keepdims=True)
+    starts_col = column_of(starts_row)
+    token_row = iota((places, tokens), 1).astype(F32)
+    begun = token_row >= starts_col
+    start_row = jnp.max(jnp.where(begun, starts_col, 0.0), axis=0, keepdims=True)
+    segment_row = jnp.sum(jnp.where(begun, 1.0, 0.0), axis=0, keepdims=True) - 1.0
+    token_col = iota((tokens, places), 0).astype(F32)
+    start_col = jnp.max(jnp.where(token_col >= starts_row, starts_row, 0.0), axis=1, keepdims=True)
+    position = iota((tokens, 1), 0).astype(F32) - start_col
+
+    h_all.finish()
+    gathered = h_buf[...].reshape(tokens, depth)
+    inner = jnp.dot(gathered, w_inner[...], preferred_element_type=F32).astype(BF16).astype(F32)
+    state = jnp.dot(gathered, w_bcdt[...], preferred_element_type=F32).astype(BF16).astype(F32)
+    gate = inner[:, :channels]
+    conv_value = silu(rolled_conv(inner[:, channels:], conv_inner[...], position))
+    conv_state = silu(rolled_conv(state[:, : 2 * NSTATE], conv_bc[...], position))
+    raw = state[:, 2 * NSTATE :] + dt_bias[...]
+    step_size = jnp.maximum(raw, 0.0) + jnp.log1p(jnp.exp(-jnp.abs(raw)))
+    first = me * channels
+    low = first // HEADDIM
+    high = (first + channels - 1) // HEADDIM
+    mask_high = (iota((1, channels), 1) + first >= high * HEADDIM).astype(F32)
+    masks = (1.0 - mask_high, mask_high)
+    steps = (pick(step_size, low), pick(step_size, high))
+    rates = (pick(decay_rate[...], low), pick(decay_rate[...], high))
+    skip = pick(d_skip[...], low) * masks[0] + pick(d_skip[...], high) * masks[1]
+    driven = conv_value * (steps[0] * masks[0] + steps[1] * masks[1])
+    lanes = iota((tokens, LANES), 1)
+    logs = jnp.where(
+        lanes == 0, -(steps[0] * rates[0]), jnp.where(lanes == 1, -(steps[1] * rates[1]), 0.0)
+    )
+    size = SCAN_BLOCK
+    causal = iota((size, size), 0) >= iota((size, size), 1)
+    lower = causal.astype(F32)
+    blocks = tokens // size
+    cuts = [slice(b * size, (b + 1) * size) for b in range(blocks)]
+    sums_col = [jnp.dot(lower, logs[cut], precision=HIGH) for cut in cuts]
+    sums_row = [jnp.transpose(s) for s in sums_col]
+    results = []
+    for b in range(blocks):
+        result = jnp.zeros((size, channels), F32)
+        for a in range(b + 1):
+            gram = lax.dot_general(
+                conv_state[cuts[b], NSTATE:], conv_state[cuts[a], :NSTATE], NT, precision=HIGH
+            )
+            same = start_col[cuts[b]] == start_row[:, cuts[a]]
+            if a == b:
+                same = same & causal
+            for slot in range(2):
+                rise = sums_col[b][:, slot : slot + 1]
+                fall = sums_row[a][slot : slot + 1, :]
+                if a == b:
+                    spread = jnp.minimum(rise - fall, 0.0)
+                else:
+                    rest = sums_col[a][size - 1 : size, slot : slot + 1] - fall
+                    for between in range(a + 1, b):
+                        rest = rest + sums_col[between][size - 1 : size, slot : slot + 1]
+                    spread = rise + jnp.minimum(rest, 0.0)
+                weights = jnp.where(same, jnp.exp(spread), 0.0)
+                result = result + jnp.dot(
+                    gram * weights, driven[cuts[a]] * masks[slot], precision=HIGH
+                )
+        results.append(result)
+    mixed = jnp.concatenate(results, axis=0) + skip * conv_value
+    gated = (mixed * silu(gate)).astype(BF16)
+    eye = (iota((channels, channels), 0) == iota((channels, channels), 1)).astype(BF16)
+    g_buf[me] = lax.dot_general(eye, gated, NT, preferred_element_type=F32).astype(BF16)
+
+    g_all = Gather(g_buf, g_z, g_p, g_c, g_r, count, me)
+    g_all.start()
+    own_columns = (iota((columns, depth), 1) == iota((columns, depth), 0) + me * columns).astype(BF16)
+    hidden_t = lax.dot_general(own_columns, gathered, NT, preferred_element_type=F32)
+    g_all.forward()
+    fetch.wait()
+    tail[...] = jnp.zeros_like(tail)
+    for k in range(depth // LANES):
+        span = slice(k * LANES, (k + 1) * LANES)
+        gain = final_gain[:, span]
+        for j in range(padded // LANES):
+            if (j + 1) * LANES <= vocab:
+                block = heads[span, j * LANES : (j + 1) * LANES].astype(F32)
+            else:
+                tail[:, : vocab - j * LANES] = heads[span, j * LANES : vocab].astype(F32)
+                block = tail[...]
+            heads_t[j * LANES : (j + 1) * LANES, span] = (jnp.transpose(block) * gain).astype(BF16)
+
+    def taken(d, carry):
+        device = (me + count - d) % count
+        remote(w_src.at[device], w_dst.at[device], w_s.at[d], w_r.at[d], device).wait_recv()
+        return carry
+
+    lax.fori_loop(1, count, taken, 0)
+    w_columns = w_dst[...].reshape(count * channels, LANES)[:, :columns]
+    g_all.finish()
+    g_t = g_buf[...].reshape(count * channels, tokens)
+    wide_g = g_t.astype(F32)
+    squares = jnp.sum(wide_g * wide_g, axis=0, keepdims=True)
+    inverse = lax.rsqrt(squares / (count * channels) + EPSILON)
+    delta = lax.dot_general(
+        w_columns, g_t, (((0,), (0,)), ((), ())), preferred_element_type=F32
+    )
+    l_buf[me] = (hidden_t + delta * inverse).astype(BF16)
+
+    l_all = Gather(l_buf, l_z, l_p, l_c, l_r, count, me)
+    l_all.start()
+    l_all.forward()
+    l_all.finish()
+    layer_t = l_buf[...].reshape(depth, tokens)
+    own_rows = (iota((rows, tokens), 1) == iota((rows, tokens), 0) + me * rows).astype(BF16)
+    layer_out[...] = lax.dot_general(own_rows, layer_t, NT, preferred_element_type=F32).astype(BF16)
+    wide_l = layer_t.astype(F32)
+    scale = lax.rsqrt(jnp.sum(wide_l * wide_l, axis=0, keepdims=True) / depth + EPSILON)
+    label = labels[...] - me * vocab
+    top = jnp.full((1, tokens), -jnp.inf, F32)
+    target = jnp.zeros((1, tokens), F32)
+    for j in range(padded // LANES):
+        piece = jnp.dot(
+            heads_t[j * LANES : (j + 1) * LANES, :], layer_t, preferred_element_type=F32
+        ) * scale
+        entry = iota((LANES, tokens), 0) + j * LANES
+        target = target + jnp.sum(
+            jnp.where(entry == jnp.where(label < vocab, label, -1), piece, 0.0), axis=0, keepdims=True
+        )
+        if (j + 1) * LANES > vocab:
+            piece = jnp.where(entry < vocab, piece, -jnp.inf)
+        scores[j * LANES : (j + 1) * LANES, :] = piece
+        top = jnp.maximum(top, jnp.max(piece, axis=0, keepdims=True))
+    total = jnp.sum(jnp.exp(scores[...] - top), axis=0, keepdims=True)
+    local = top + jnp.log(total)
+    parts = tokens // LANES
+    for i in range(parts):
+        f_buf[me, i : i + 1, :] = local[:, i * LANES : (i + 1) * LANES]
+        f_buf[me, parts + i : parts + i + 1, :] = target[:, i * LANES : (i + 1) * LANES]
+
+    def tell(d, carry):
+        device = (me + d) % count
+        remote(f_buf.at[me], f_buf.at[me], f_s.at[d], f_r.at[d], device).start()
+        return carry
+
+    lax.fori_loop(1, count, tell, 0)
+
+    for gather in (h_all, g_all, l_all):
+        gather.drain()
+
+    def heard(d, carry):
+        device = (me + count - d) % count
+        remote(f_buf.at[device], f_buf.at[device], f_s.at[d], f_r.at[d], device).wait_recv()
+        return carry
+
+    lax.fori_loop(1, count, heard, 0)
+    every = f_buf[...]
+    ends = every[:, :parts, :]
+    peak = jnp.max(ends, axis=0)
+    norm = peak + jnp.log(jnp.sum(jnp.exp(ends - peak[None]), axis=0))
+    square = jnp.sum(every[:, parts:, :], axis=0) - norm
+    logprob = jnp.concatenate([square[i : i + 1, :] for i in range(parts)], axis=1)
+    token_out[...] = lax.dot_general(
+        jnp.broadcast_to(logprob, (8, tokens)), own_rows.astype(F32), NT, precision=HIGH
+    )[0:1, :]
+    member = iota((places, tokens), 0).astype(F32) == segment_row
+    sums = jnp.sum(jnp.where(member, logprob, 0.0), axis=1, keepdims=True)
+    owner_col = column_of(owners[...].astype(F32))
+    slots = iota((places, places), 1).astype(F32) == owner_col
+    seq_out[...] = jnp.sum(jnp.where(slots, sums, 0.0), axis=0, keepdims=True)
+
+    def sent(d, carry):
+        remote(w_src.at[me], w_dst.at[me], w_s.at[d], w_r.at[d], h_all.sibling).wait_send()
+        remote(f_buf.at[me], f_buf.at[me], f_s.at[d], f_r.at[d], h_all.sibling).wait_send()
+        return carry
+
+    lax.fori_loop(1, count, sent, 0)
+
+
+def fused(
+    hidden,
+    labels,
+    lengths,
+    owners,
+    w_inner,
+    w_bcdt,
+    conv_inner,
+    conv_bc,
+    dt_bias,
+    decay_rate,
+    d_skip,
+    norm_gain,
+    w_out,
+    final_gain,
+    w_head,
+):
+    count = lax.axis_size("blk")
+    rows, depth = hidden.shape[1:]
+    tokens = rows * count
+    channels = w_inner.shape[2]
+    vocab = w_head.shape[1]
+    padded = -(-vocab // LANES) * LANES
+    width = count // (2 * PLANES)
+    vmem = pl.BlockSpec(memory_space=pltpu.VMEM)
+    gather_sems = [
+        pltpu.SemaphoreType.DMA((PLANES - 1,)),
+        pltpu.SemaphoreType.DMA((PLANES * (width - 1),)),
+        pltpu.SemaphoreType.DMA((PLANES * width,)),
+        pltpu.SemaphoreType.DMA((count,)),
+    ]
+    layer, token, seq = pl.pallas_call(
+        functools.partial(kernel, count),
+        out_shape=(
+            jax.ShapeDtypeStruct((rows, depth), BF16),
+            jax.ShapeDtypeStruct((1, rows), F32),
+            jax.ShapeDtypeStruct((1, owners.shape[0]), F32),
+        ),
+        in_specs=[vmem] * 14 + [pl.BlockSpec(memory_space=pl.ANY)],
+        out_specs=(vmem, vmem, vmem),
+        scratch_shapes=[
+            pltpu.VMEM((count, rows, depth), BF16),
+            pltpu.VMEM((count, channels, tokens), BF16),
+            pltpu.VMEM((count, depth // count, tokens), BF16),
+            pltpu.VMEM((count, channels, LANES), BF16),
+            pltpu.VMEM((count, channels, LANES), BF16),
+            pltpu.VMEM((count, 2 * tokens // LANES, LANES), F32),
+            pltpu.VMEM((channels, depth), F32),
+            pltpu.VMEM((depth, vocab), BF16),
+            pltpu.VMEM((LANES, LANES), F32),
+            pltpu.VMEM((padded, depth), BF16),
+            pltpu.VMEM((padded, tokens), F32),
+        ]
+        + gather_sems * 3
+        + [pltpu.SemaphoreType.DMA((count,))] * 4
+        + [pltpu.SemaphoreType.DMA],
+        compiler_params=pltpu.CompilerParams(
+            collective_id=0, has_side_effects=True, vmem_limit_bytes=56 * 1024 * 1024
+        ),
+    )(
+        hidden[0],
+        labels,
+        lengths,
+        owners.reshape(1, -1),
+        w_inner.reshape(depth, 2 * channels),
+        w_bcdt,
+        conv_inner,
+        conv_bc,
+        dt_bias.reshape(1, -1),
+        decay_rate.reshape(1, -1),
+        d_skip.reshape(1, -1),
+        norm_gain.reshape(1, -1),
+        w_out,
+        final_gain.reshape(1, -1),
+        w_head,
+    )
+    return (layer[None], token, seq[0])
+
+
+def layer(*args):
+    hidden, w_inner = args[0], args[4]
+    count = lax.axis_size("blk")
+    rows, depth = hidden.shape[1:]
+    tokens = rows * count
+    whole = lax.axis_size("seq") == 1 and count % (4 * PLANES) == 0
+    tiled = rows % 16 == 0 and w_inner.shape[2] % 16 == 0 and depth % (16 * count) == 0
+    sized = depth // count <= LANES and tokens % SCAN_BLOCK == 0 and depth % LANES == 0
+    return (fused if whole and tiled and sized else shards)(*args)
+
+
 def solution(mesh):
     in_specs = (
         P(("mp", "seq"), "blk", None),
@@ -206,4 +688,4 @@
         P("mp", "blk"),
     )
     out_specs = (P(("mp", "seq"), "blk", None), P(("mp", "seq"), "blk"), P(("mp", "seq")))
-    return jax.shard_map(shards, mesh=mesh, in_specs=in_specs, out_specs=out_specs, check_vma=False)
+    return jax.shard_map(layer, mesh=mesh, in_specs=in_specs, out_specs=out_specs, check_vma=False)

time: 396 us -> 83.4 us (0.21)
  waiting for transfers between devices: 205 us -> 0 us
  blocking collectives: 118 us -> 0 us
  Pallas kernels: 0 us -> 70.3 us
  other arithmetic: 21.6 us -> 0 us
  matrix products: 16.3 us -> 0 us
  between operations: 14 us -> 0.65 us
  loops' own time: 5.61 us -> 0 us
    all_gather x2 -> x0, waiting for transfers between devices: 103 us -> none  [the longest x1 55 us: shards(): lax.all_gather(final_norm(layer_own, final_gain), 'blk', axis=0, tiled=True)]
    reduce_scatter x1 -> x0, waiting for transfers between devices: 102 us -> none  [shards(): lax.psum_scatter(jnp.dot(gated_norm, w_out, preferred_element_type=jnp.fl...]
    psum x2 -> x0, blocking collectives: 79.2 us -> none  [the longest x1 40.3 us: shards(): expsum_all, target_all = lax.psum((expsum_local, target_local), 'blk')]
    pallas_call x0 -> x1, Pallas kernels: none -> 70.3 us  [fused(): pl.pallas_call(functools.partial(kernel, count), out_shape=(jax.ShapeDtyp...]
    pmax x1 -> x0, blocking collectives: 38.8 us -> none  [shards(): top_all = lax.pmax(top_local, 'blk')]
    dot_general x16 -> x0, matrix products: 16.3 us -> none  [the longest x1 4.05 us: shards(): jnp.dot(lax.all_gather(final_norm(layer_own, final_gain), 'blk', axis=0,...]
    unnamed x17 -> x7, local copies, waits for them, and re-layouts: 1.18 us -> 8.84 us
    another operation x1 -> x0, loops' own time: 5.61 us -> none  [shards(): final_carry, scanned = lax.scan(block_step, initial, scan_inputs)]
  transfers between devices with their start and end apart: 3 -> 0, of which waited for: 3 -> 0; matrix products, arithmetic and copies ran while one was open for 3% -> 0% of each run, Pallas kernels for 0% -> 0%
where the time goes in v1:
time: 83.4 us; the launch traced here: 83.1 us
  Pallas kernels  70.3 us (84%)
  local copies, waits for them, and re-layouts  12.2 us (15%)
    pallas_call x1, Pallas kernels, fused(): pl.pallas_call(functools.partial(kernel, count), out_shape=(jax.ShapeDtyp...  70.3 us
    unnamed x7, local copies, waits for them, and re-layouts  8.84 us
    reshape x1, local copies, waits for them, and re-layouts, fused(): w_inner.reshape(depth, 2 * channels)  1.89 us

profile of v1, /device:TPU:0, one launch (start us, length us, event | category | flops | bytes accessed | tf_op | source)
XLA Modules:
  0.0 83.1 jit_solution(11950914020207917500)
XLA Ops:
  0.6 0.0 copy-start
  0.6 1.4 %reshape.33.final_gain = f32[1,1536]{1,0:T(1,128)} reshape(f32[1536]{0:T(1024)} %param.28) | data formatting | bytes 12288 | tf_op jit(solution)/shard_map/reshape | solution.py:655
  2.1 1.9 %copy.21.w_inner = bf16[1536,96]{1,0:T(8,128)(2,1)} copy(bf16[1536,96]{0,1:T(8,128)(2,1)} %bitcast.9) | data formatting | bytes 589824 | tf_op jit(solution)/shard_map/reshape | solution.py:646
  4.0 2.3 %copy.22.w_bcdt = bf16[1536,280]{1,0:T(8,128)(2,1)} copy(bf16[1536,280]{0,1:T(8,128)(2,1)} %param.20) | data formatting | bytes 1720320 | tf_op args[5]
  6.3 0.0 copy-done
  6.3 2.7 %copy.23.w_head = bf16[1536,786]{1,0:T(8,128)(2,1)} copy(bf16[1536,786]{0,1:T(8,128)(2,1)S(1)} %copy-done) | data formatting | bytes 4829184 | tf_op args[14]
  9.0 70.3 %shard_map.166 = (bf16[16,1536]{1,0:T(8,128)(2,1)}, f32[1,16]{1,0:T(1,128)}, f32[1,8]{1,0:T(1,128)}) custom-call(bf16[16,1536]{1,0:T(8,128)(2,1)} %bitcast.10, s32[1,512]{1,0:T(1,128)} %labels.1, s32[1,8]{1,0:T(1,128)} %lengths.1, s32[1,8]{1,0:T(1,128)} %bitcast.12, bf16[1536,96]{1,0:T(8,128)(2,1)} %copy.21.w_inner, bf16[1536,280]{1,0:T(8,128)(2,1)} %copy.22.w_bcdt, ...), custom_call_target="tpu_custom_call" | custom-call | tf_op jit(solution)/shard_map/pallas_call | solution.py:613
  79.3 1.4 %copy.27 = bf16[1,16,1536]{2,1,0:T(8,128)(2,1)} copy(bf16[1,16,1536]{2,1,0:T(8,128)(2,1)} %bitcast.11) | data formatting | bytes 98304
  80.8 1.2 %copy.28 = f32[1,16]{1,0:T(1,128)} copy(f32[1,16]{1,0:T(1,128)} %get-tuple-element.13) | data formatting | bytes 128
  82.0 1.2 %copy.29 = f32[8]{0:T(128)} copy(f32[8]{0:T(128)} %bitcast.17) | data formatting | bytes 64
Async XLA Ops:
  0.6 5.7 %copy-start = (bf16[1536,786]{0,1:T(8,128)(2,1)S(1)}, bf16[1536,786]{0,1:T(8,128)(2,1)}, u32[]{:S(2)}) copy-start(bf16[1536,786]{0,1:T(8,128)(2,1)} %param.29) | copy-start | bytes 7243780

commit v2 on v1

--- a/solution.py
+++ b/solution.py
@@ -317,6 +317,15 @@
     return jnp.sum(jnp.where(lanes == index, row, 0.0), axis=1, keepdims=True)
 
 
+def split(values, number):
+    parts = []
+    for _ in range(number):
+        part = values.astype(BF16)
+        parts.append(part)
+        values = values - part.astype(F32)
+    return parts
+
+
 def column_of(row):
     size = row.shape[1]
     same = iota((size, size), 0) == iota((size, size), 1)
@@ -351,7 +360,6 @@
     f_buf,
     wide,
     heads,
-    tail,
     heads_t,
     scores,
     h_z, h_p, h_c, h_r,
@@ -365,9 +373,9 @@
     rows = hidden.shape[0]
     depth = hidden.shape[1]
     tokens = rows * count
-    channels = w_inner.shape[1] // 2
+    channels = w_inner.shape[0] // 2
     columns = depth // count
-    vocab = w_head.shape[1]
+    vocab = w_head.shape[0]
     padded = heads_t.shape[0]
 
     fetch = pltpu.make_async_copy(w_head, heads, head_sem)
@@ -417,8 +425,10 @@
 
     h_all.finish()
     gathered = h_buf[...].reshape(tokens, depth)
-    inner = jnp.dot(gathered, w_inner[...], preferred_element_type=F32).astype(BF16).astype(F32)
-    state = jnp.dot(gathered, w_bcdt[...], preferred_element_type=F32).astype(BF16).astype(F32)
+    inner = lax.dot_general(gathered, w_inner[...], NT, preferred_element_type=F32)
+    inner = inner.astype(BF16).astype(F32)
+    state = lax.dot_general(gathered, w_bcdt[...], NT, preferred_element_type=F32)
+    state = state.astype(BF16).astype(F32)
     gate = inner[:, :channels]
     conv_value = silu(rolled_conv(inner[:, channels:], conv_inner[...], position))
     conv_state = silu(rolled_conv(state[:, : 2 * NSTATE], conv_bc[...], position))
@@ -439,17 +449,27 @@
     )
     size = SCAN_BLOCK
     causal = iota((size, size), 0) >= iota((size, size), 1)
-    lower = causal.astype(F32)
+    lower = causal.astype(BF16)
+    in_parts = split(conv_state[:, :NSTATE], 2)
+    out_parts = split(conv_state[:, NSTATE:], 2)
+    drive_parts = split(driven, 2)
     blocks = tokens // size
     cuts = [slice(b * size, (b + 1) * size) for b in range(blocks)]
-    sums_col = [jnp.dot(lower, logs[cut], precision=HIGH) for cut in cuts]
+    log_parts = split(logs, 3)
+    sums_col = [
+        sum(jnp.dot(lower, part[cut], preferred_element_type=F32) for part in log_parts)
+        for cut in cuts
+    ]
     sums_row = [jnp.transpose(s) for s in sums_col]
     results = []
     for b in range(blocks):
         result = jnp.zeros((size, channels), F32)
         for a in range(b + 1):
-            gram = lax.dot_general(
-                conv_state[cuts[b], NSTATE:], conv_state[cuts[a], :NSTATE], NT, precision=HIGH
+            gram = sum(
+                lax.dot_general(
+                    out_parts[i][cuts[b]], in_parts[j][cuts[a]], NT, preferred_element_type=F32
+                )
+                for i, j in ((0, 1), (1, 0), (0, 0))
             )
             same = start_col[cuts[b]] == start_row[:, cuts[a]]
             if a == b:
@@ -465,9 +485,12 @@
                         rest = rest + sums_col[between][size - 1 : size, slot : slot + 1]
                     spread = rise + jnp.minimum(rest, 0.0)
                 weights = jnp.where(same, jnp.exp(spread), 0.0)
-                result = result + jnp.dot(
-                    gram * weights, driven[cuts[a]] * masks[slot], precision=HIGH
+                mix_parts = split(gram * weights, 2)
+                share = sum(
+                    jnp.dot(mix_parts[i], drive_parts[j][cuts[a]], preferred_element_type=F32)
+                    for i, j in ((0, 1), (1, 0), (0, 0))
                 )
+                result = result + share * masks[slot]
         results.append(result)
     mixed = jnp.concatenate(results, axis=0) + skip * conv_value
     gated = (mixed * silu(gate)).astype(BF16)
@@ -480,17 +503,11 @@
     hidden_t = lax.dot_general(own_columns, gathered, NT, preferred_element_type=F32)
     g_all.forward()
     fetch.wait()
-    tail[...] = jnp.zeros_like(tail)
+    heads_t[padded - LANES :, :] = jnp.zeros((LANES, depth), BF16)
     for k in range(depth // LANES):
         span = slice(k * LANES, (k + 1) * LANES)
-        gain = final_gain[:, span]
-        for j in range(padded // LANES):
-            if (j + 1) * LANES <= vocab:
-                block = heads[span, j * LANES : (j + 1) * LANES].astype(F32)
-            else:
-                tail[:, : vocab - j * LANES] = heads[span, j * LANES : vocab].astype(F32)
-                block = tail[...]
-            heads_t[j * LANES : (j + 1) * LANES, span] = (jnp.transpose(block) * gain).astype(BF16)
+        gain = final_gain[k : k + 1, :]
+        heads_t[0:vocab, span] = (heads[:, span].astype(F32) * gain).astype(BF16)
 
     def taken(d, carry):
         device = (me + count - d) % count
@@ -627,8 +644,7 @@
             pltpu.VMEM((count, channels, LANES), BF16),
             pltpu.VMEM((count, 2 * tokens // LANES, LANES), F32),
             pltpu.VMEM((channels, depth), F32),
-            pltpu.VMEM((depth, vocab), BF16),
-            pltpu.VMEM((LANES, LANES), F32),
+            pltpu.VMEM((vocab, depth), BF16),
             pltpu.VMEM((padded, depth), BF16),
             pltpu.VMEM((padded, tokens), F32),
         ]
@@ -643,8 +659,8 @@
         labels,
         lengths,
         owners.reshape(1, -1),
-        w_inner.reshape(depth, 2 * channels),
-        w_bcdt,
+        w_inner.transpose(1, 2, 0).reshape(2 * channels, depth),
+        w_bcdt.T,
         conv_inner,
         conv_bc,
         dt_bias.reshape(1, -1),
@@ -652,8 +668,8 @@
         d_skip.reshape(1, -1),
         norm_gain.reshape(1, -1),
         w_out,
-        final_gain.reshape(1, -1),
-        w_head,
+        final_gain.reshape(-1, LANES),
+        w_head.T,
     )
     return (layer[None], token, seq[0])
 

time: 83.4 us -> 74.8 us (0.90)
  local copies, waits for them, and re-layouts: 12.2 us -> 3.68 us
    unnamed x7 -> x3, local copies, waits for them, and re-layouts: 8.84 us -> 3.68 us
    reshape x2 -> x0, local copies, waits for them, and re-layouts: 3.33 us -> none  [the longest x1 1.89 us: fused(): w_inner.reshape(depth, 2 * channels)]
where the time goes in v2:
time: 74.8 us; the launch traced here: 74.6 us
  Pallas kernels  70.3 us (94%)
  local copies, waits for them, and re-layouts  3.68 us (5%)
    pallas_call x1, Pallas kernels, fused(): pl.pallas_call(functools.partial(kernel, count), out_shape=(jax.ShapeDtyp...  70.3 us
    unnamed x3, local copies, waits for them, and re-layouts  3.68 us

profile of v2, /device:TPU:0, one launch (start us, length us, event | category | flops | bytes accessed | tf_op | source)
XLA Modules:
  0.0 74.6 jit_solution(1624421714475398135)
XLA Ops:
  0.6 70.3 %shard_map.166 = (bf16[16,1536]{1,0:T(8,128)(2,1)}, f32[1,16]{1,0:T(1,128)}, f32[1,8]{1,0:T(1,128)}) custom-call(bf16[16,1536]{1,0:T(8,128)(2,1)} %bitcast.17, s32[1,512]{1,0:T(1,128)} %labels.1, s32[1,8]{1,0:T(1,128)} %lengths.1, s32[1,8]{1,0:T(1,128)} %bitcast.20, bf16[96,1536]{1,0:T(8,128)(2,1)} %bitcast.16, bf16[280,1536]{1,0:T(8,128)(2,1)} %bitcast.15, ...), custom_call_target="tpu_custom_call" | custom-call | tf_op jit(solution)/shard_map/pallas_call | solution.py:630
  70.9 1.4 %copy.21 = bf16[1,16,1536]{2,1,0:T(8,128)(2,1)} copy(bf16[1,16,1536]{2,1,0:T(8,128)(2,1)} %bitcast.18) | data formatting | bytes 98304
  72.4 1.1 %copy.22 = f32[1,16]{1,0:T(1,128)} copy(f32[1,16]{1,0:T(1,128)} %get-tuple-element.13) | data formatting | bytes 128
  73.5 1.1 %copy.23 = f32[8]{0:T(128)} copy(f32[8]{0:T(128)} %bitcast.25) | data formatting | bytes 64

commit v3 on v2

--- a/solution.py
+++ b/solution.py
@@ -231,7 +231,15 @@
         return remote(self.buf.at[block], self.buf.at[block], send_sem, self.recv_sem.at[block], device)
 
     def plane_at(self, step):
-        return (self.plane + step) % self.planes
+        half = self.planes // 2
+        upper = self.plane // half
+        last = self.planes - 1
+        mine = self.plane + upper * (last - 2 * self.plane)
+        rank = step - 1
+        other = rank + (rank - mine + self.planes) // self.planes
+        other = other + upper * (last - 2 * other)
+        away = (step + last) // self.planes
+        return self.plane + away * (other - self.plane)
 
     def spot_at(self, step):
         return (self.spot + step) % self.width
@@ -401,14 +409,6 @@
         w_src[e, :, 0:columns] = wide[:, e * columns : (e + 1) * columns].astype(BF16)
     h_all.forward()
 
-    def give(d, carry):
-        device = (me + d) % count
-        remote(w_src.at[device], w_dst.at[me], w_s.at[d], w_r.at[d], device).start()
-        return carry
-
-    lax.fori_loop(1, count, give, 0)
-    w_dst[me] = w_src[me]
-
     places = lengths.shape[1]
     length_row = lengths[...].astype(F32)
     length_col = column_of(length_row)
@@ -424,6 +424,15 @@
     position = iota((tokens, 1), 0).astype(F32) - start_col
 
     h_all.finish()
+
+    def give(d, carry):
+        device = (me + d) % count
+        remote(w_src.at[device], w_dst.at[me], w_s.at[d], w_r.at[d], device).start()
+        return carry
+
+    lax.fori_loop(1, count, give, 0)
+    w_dst[me] = w_src[me]
+
     gathered = h_buf[...].reshape(tokens, depth)
     inner = lax.dot_general(gathered, w_inner[...], NT, preferred_element_type=F32)
     inner = inner.astype(BF16).astype(F32)
@@ -531,8 +540,6 @@
     l_all.forward()
     l_all.finish()
     layer_t = l_buf[...].reshape(depth, tokens)
-    own_rows = (iota((rows, tokens), 1) == iota((rows, tokens), 0) + me * rows).astype(BF16)
-    layer_out[...] = lax.dot_general(own_rows, layer_t, NT, preferred_element_type=F32).astype(BF16)
     wide_l = layer_t.astype(F32)
     scale = lax.rsqrt(jnp.sum(wide_l * wide_l, axis=0, keepdims=True) / depth + EPSILON)
     label = labels[...] - me * vocab
@@ -564,6 +571,8 @@
 
     lax.fori_loop(1, count, tell, 0)
 
+    own_rows = (iota((rows, tokens), 1) == iota((rows, tokens), 0) + me * rows).astype(BF16)
+    layer_out[...] = lax.dot_general(own_rows, layer_t, NT, preferred_element_type=F32).astype(BF16)
     for gather in (h_all, g_all, l_all):
         gather.drain()
 

time: 74.8 us -> 71.5 us (0.956)
  Pallas kernels: 70.3 us -> 66.4 us
    pallas_call x1, Pallas kernels: 70.3 us -> 66.4 us  [fused(): pl.pallas_call(functools.partial(kernel, count), out_shape=(jax.ShapeDtyp...]
where the time goes in v3:
time: 71.5 us; the launch traced here: 70.7 us
  Pallas kernels  66.4 us (93%)
  local copies, waits for them, and re-layouts  3.68 us (5%)
    pallas_call x1, Pallas kernels, fused(): pl.pallas_call(functools.partial(kernel, count), out_shape=(jax.ShapeDtyp...  66.4 us
    unnamed x3, local copies, waits for them, and re-layouts  3.68 us

profile of v3, /device:TPU:0, one launch (start us, length us, event | category | flops | bytes accessed | tf_op | source)
XLA Modules:
  0.0 70.7 jit_solution(4542047508564566143)
XLA Ops:
  0.6 66.4 %shard_map.166 = (bf16[16,1536]{1,0:T(8,128)(2,1)}, f32[1,16]{1,0:T(1,128)}, f32[1,8]{1,0:T(1,128)}) custom-call(bf16[16,1536]{1,0:T(8,128)(2,1)} %bitcast.17, s32[1,512]{1,0:T(1,128)} %labels.1, s32[1,8]{1,0:T(1,128)} %lengths.1, s32[1,8]{1,0:T(1,128)} %bitcast.20, bf16[96,1536]{1,0:T(8,128)(2,1)} %bitcast.16, bf16[280,1536]{1,0:T(8,128)(2,1)} %bitcast.15, ...), custom_call_target="tpu_custom_call" | custom-call | tf_op jit(solution)/shard_map/pallas_call | solution.py:639
  67.0 1.4 %copy.21 = bf16[1,16,1536]{2,1,0:T(8,128)(2,1)} copy(bf16[1,16,1536]{2,1,0:T(8,128)(2,1)} %bitcast.18) | data formatting | bytes 98304
  68.4 1.1 %copy.22 = f32[1,16]{1,0:T(1,128)} copy(f32[1,16]{1,0:T(1,128)} %get-tuple-element.13) | data formatting | bytes 128
  69.6 1.1 %copy.23 = f32[8]{0:T(128)} copy(f32[8]{0:T(128)} %bitcast.25) | data formatting | bytes 64

commit v4 on v3

--- a/solution.py
+++ b/solution.py
@@ -241,16 +241,16 @@
         away = (step + last) // self.planes
         return self.plane + away * (other - self.plane)
 
-    def spot_at(self, step):
-        return (self.spot + step) % self.width
+    def beside(self, d):
+        x, y = self.spot % 2, self.spot // 2
+        along_x, along_y = self.spot + 1 - 2 * x, self.spot + 2 - 4 * y
+        first = along_x + self.core * (along_y - along_x)
+        return (first, along_x + along_y - first, self.width - 1 - self.spot)[d]
 
     def to_plane(self, block, step):
-        def one(d, carry):
-            device = self.index(self.plane, self.spot_at(d), self.core)
-            self.copy(block, self.p_sem.at[step * (self.width - 1) + d - 1], device).start()
-            return carry
-
-        lax.fori_loop(1, self.width, one, 0)
+        for d in range(2):
+            device = self.index(self.plane, self.beside(d), self.core)
+            self.copy(block, self.p_sem.at[step * (self.width - 1) + d], device).start()
 
     def to_core(self, block, slot):
         self.copy(block, self.c_sem.at[slot], self.sibling).start()
@@ -268,24 +268,34 @@
     def arrived(self, block):
         self.copy(block, self.c_sem.at[0], self.sibling).wait_recv()
 
+    def receive(self, step, d):
+        block = self.index(self.plane_at(step), self.beside(d), self.core)
+        self.arrived(block)
+        slot = step * (self.width - 1) + d
+        if d == 0:
+            device = self.index(self.plane, self.beside(1), self.core)
+            self.copy(block, self.p_sem.at[step * (self.width - 1) + 2], device).start()
+        self.to_core(block, self.planes + slot)
+
     def forward(self):
-        def along(d, carry):
-            block = self.index(self.plane_at(d), self.spot, self.core)
+        def along(step, carry):
+            block = self.index(self.plane_at(step), self.spot, self.core)
             self.arrived(block)
-            self.to_plane(block, d)
-            self.to_core(block, d)
+            self.to_plane(block, step)
+            self.to_core(block, step)
+            self.receive(step - 1, 0)
+            self.receive(step - 1, 1)
             return carry
 
         lax.fori_loop(1, self.planes, along, 0)
-
-        def within(i, carry):
-            step, d = i // (self.width - 1), i % (self.width - 1) + 1
-            block = self.index(self.plane_at(step), self.spot_at(d), self.core)
-            self.arrived(block)
-            self.to_core(block, self.planes + i)
+        self.receive(self.planes - 1, 0)
+        self.receive(self.planes - 1, 1)
+
+        def across(step, carry):
+            self.receive(step, 2)
             return carry
 
-        lax.fori_loop(0, self.planes * (self.width - 1), within, 0)
+        lax.fori_loop(0, self.planes, across, 0)
 
     def finish(self):
         def last(i, carry):
@@ -688,7 +698,7 @@
     count = lax.axis_size("blk")
     rows, depth = hidden.shape[1:]
     tokens = rows * count
-    whole = lax.axis_size("seq") == 1 and count % (4 * PLANES) == 0
+    whole = lax.axis_size("seq") == 1 and count == 8 * PLANES
     tiled = rows % 16 == 0 and w_inner.shape[2] % 16 == 0 and depth % (16 * count) == 0
     sized = depth // count <= LANES and tokens % SCAN_BLOCK == 0 and depth % LANES == 0
     return (fused if whole and tiled and sized else shards)(*args)

time: 71.5 us -> 76.1 us (1.064)
  Pallas kernels: 66.4 us -> 71.6 us
    pallas_call x1, Pallas kernels: 66.4 us -> 71.6 us  [fused(): pl.pallas_call(functools.partial(kernel, count), out_shape=(jax.ShapeDtyp...]
where the time goes in v4:
time: 76.1 us; the launch traced here: 75.9 us
  Pallas kernels  71.6 us (94%)
  local copies, waits for them, and re-layouts  3.68 us (5%)
    pallas_call x1, Pallas kernels, fused(): pl.pallas_call(functools.partial(kernel, count), out_shape=(jax.ShapeDtyp...  71.6 us
    unnamed x3, local copies, waits for them, and re-layouts  3.68 us

profile of v4, /device:TPU:0, one launch (start us, length us, event | category | flops | bytes accessed | tf_op | source)
XLA Modules:
  0.0 75.9 jit_solution(2367728988942200069)
XLA Ops:
  0.6 71.6 %shard_map.166 = (bf16[16,1536]{1,0:T(8,128)(2,1)}, f32[1,16]{1,0:T(1,128)}, f32[1,8]{1,0:T(1,128)}) custom-call(bf16[16,1536]{1,0:T(8,128)(2,1)} %bitcast.17, s32[1,512]{1,0:T(1,128)} %labels.1, s32[1,8]{1,0:T(1,128)} %lengths.1, s32[1,8]{1,0:T(1,128)} %bitcast.20, bf16[96,1536]{1,0:T(8,128)(2,1)} %bitcast.16, bf16[280,1536]{1,0:T(8,128)(2,1)} %bitcast.15, ...), custom_call_target="tpu_custom_call" | custom-call | tf_op jit(solution)/shard_map/pallas_call | solution.py:649
  72.2 1.4 %copy.21 = bf16[1,16,1536]{2,1,0:T(8,128)(2,1)} copy(bf16[1,16,1536]{2,1,0:T(8,128)(2,1)} %bitcast.18) | data formatting | bytes 98304
  73.6 1.1 %copy.22 = f32[1,16]{1,0:T(1,128)} copy(f32[1,16]{1,0:T(1,128)} %get-tuple-element.13) | data formatting | bytes 128
  74.8 1.1 %copy.23 = f32[8]{0:T(128)} copy(f32[8]{0:T(128)} %bitcast.25) | data formatting | bytes 64
